TPU v7x, 32 devices: a whole 2x2x4 slice. The times are simulated.
32 devices in a mesh: groups: 2 (over y), row: 4 (over z), col: 4 (over x, core).
Axes of the slice: x: 2, y: 2, z: 4, core: 2. Of those that a mesh axis runs over, the one named last changes fastest.
Arguments:
- pair: bfloat16 [128, 64, 128], P(('groups', 'row'), 'col'), parts along dimension 0, may hold values from -6 to 6
- pair_cotangent: bfloat16 [128, 64, 128], P(('groups', 'row'), 'col'), parts along dimension 0, may hold values from -6 to 6
- edge_weights: bfloat16 [2, 128, 640], replicated, may hold values from -0.5 to 0.5
- out_weights: bfloat16 [2, 128, 128], replicated, may hold values from -0.5 to 0.5
- norm_gains: float32 [2, 2, 128], replicated, may hold values from 0.1 to 1.9
- norm_shifts: float32 [2, 2, 128], replicated, may hold values from -3 to 3
Outputs:
- pair_grad: bfloat16 [128, 64, 128], P(('groups', 'row'), 'col'), parts along dimension 0
- edge_grads: bfloat16 [4, 128, 64, 128], P(None, ('groups', 'row'), 'col'), parts along dimension 1
There are 2 independent parts, one for each index of `groups`. A program takes and returns all parts, laid end to end along the dimension named above; an argument that names none is the same for every part. Nothing has to cross between parts.
All inputs are finite; a program needn't handle non-finite values.
Results may differ from a plain program's by a relative error of at most 0.012.
Values may be sent and summed in bfloat16 or wider, within the bound.
A program may use at most 128 MiB of HBM per device.

v0:
```python
import jax
import jax.numpy as jnp
from jax import lax
from jax.sharding import PartitionSpec as P

EPSILON = 1e-05


def product_of(form, left, right):
    return jnp.einsum(form, left, right, preferred_element_type=jnp.float32)


def layer_norm(inputs, norm_gain, norm_shift):
    centre = jnp.mean(inputs, axis=-1, keepdims=True)
    centred = inputs - centre
    inverse = lax.rsqrt(jnp.mean(centred * centred, axis=-1, keepdims=True) + EPSILON)
    standard = centred * inverse
    return (standard, inverse, standard * norm_gain + norm_shift)


def norm_backward(upstream, standard, inverse, norm_gain):
    scaled = upstream * norm_gain
    mean_grad = jnp.mean(scaled, axis=-1, keepdims=True)
    second = jnp.mean(scaled * standard, axis=-1, keepdims=True)
    return (scaled - mean_grad - standard * second) * inverse


def edges_forward(inputs, weights, norm_gain, norm_shift):
    standard, inverse, normed = layer_norm(inputs, norm_gain, norm_shift)
    projected = product_of("ijc,cd->ijd", normed.astype(jnp.bfloat16), weights)
    width = weights.shape[1] // 5
    value_left = projected[..., :width]
    sigma_left = jax.nn.sigmoid(projected[..., width : 2 * width])
    value_right = projected[..., 2 * width : 3 * width]
    sigma_right = jax.nn.sigmoid(projected[..., 3 * width : 4 * width])
    out_gate = jax.nn.sigmoid(projected[..., 4 * width :])
    left_edge = (sigma_left * value_left).astype(jnp.bfloat16)
    right_edge = (sigma_right * value_right).astype(jnp.bfloat16)
    saved = (standard, inverse, value_left, sigma_left, value_right, sigma_right, out_gate)
    return (left_edge, right_edge, saved)


def output_forward(product, out_weight, norm_gain, norm_shift):
    standard, inverse, normed = layer_norm(product, norm_gain, norm_shift)
    hidden_out = product_of("ijd,dc->ijc", normed.astype(jnp.bfloat16), out_weight)
    return (hidden_out, standard, inverse)


def output_backward(upstream, out_weight, norm_gain, out_gate, stats):
    hidden_out, standard, inverse = stats
    grad_hidden = (upstream * out_gate).astype(jnp.bfloat16)
    gate_term = upstream * hidden_out * out_gate * (1.0 - out_gate)
    grad_normed = product_of("ijc,dc->ijd", grad_hidden, out_weight)
    grad_product = norm_backward(grad_normed, standard, inverse, norm_gain).astype(jnp.bfloat16)
    return (grad_product, gate_term)


def edges_backward(grad_left, grad_right, gate_term, weights, norm_gain, saved):
    standard, inverse, value_left, sigma_left, value_right, sigma_right, out_gate = saved
    pieces = jnp.concatenate(
        [
            grad_left * sigma_left,
            grad_left * value_left * sigma_left * (1.0 - sigma_left),
            grad_right * sigma_right,
            grad_right * value_right * sigma_right * (1.0 - sigma_right),
            gate_term,
        ],
        axis=-1,
    )
    grad_normed = product_of("ijd,cd->ijc", pieces.astype(jnp.bfloat16), weights)
    return norm_backward(grad_normed, standard, inverse, norm_gain)


def row_strip(tile):
    return lax.all_gather(tile, "col", axis=1, tiled=True)


def column_strip(tile):
    return lax.all_gather(tile, "row", axis=0, tiled=True)


def shuffle_rows(tile):
    return lax.all_to_all(tile, "row", split_axis=1, concat_axis=0, tiled=True)


def shuffle_columns(tile):
    return lax.all_to_all(tile, "col", split_axis=0, concat_axis=1, tiled=True)


def transposed_columns(tile):
    row_devices = lax.axis_size("row")
    column_devices = lax.axis_size("col")
    moved = shuffle_columns(shuffle_rows(tile))
    gathered = column_strip(jnp.swapaxes(moved, 0, 1))
    total = gathered.shape[0]
    block = total // (row_devices * column_devices)
    gathered = gathered.reshape(
        row_devices, column_devices, block, gathered.shape[1], gathered.shape[2]
    )
    return jnp.swapaxes(gathered, 0, 1).reshape(total, gathered.shape[3], gathered.shape[4])


def transposed_rows(tile):
    row_devices = lax.axis_size("row")
    column_devices = lax.axis_size("col")
    moved = shuffle_rows(shuffle_columns(tile))
    gathered = row_strip(jnp.swapaxes(moved, 0, 1))
    total = gathered.shape[1]
    block = total // (row_devices * column_devices)
    gathered = gathered.reshape(
        gathered.shape[0], column_devices, row_devices, block, gathered.shape[2]
    )
    return jnp.swapaxes(gathered, 1, 2).reshape(gathered.shape[0], total, gathered.shape[4])


def body(pair, pair_cotangent, edge_weights, out_weights, norm_gains, norm_shifts):
    pair_float = pair.astype(jnp.float32)
    left_out, right_out, saved_out = edges_forward(
        pair_float, edge_weights[0], norm_gains[0, 0], norm_shifts[0, 0]
    )
    strip_right = column_strip(right_out)
    product_out = product_of("ikc,kjc->ijc", row_strip(left_out), transposed_columns(right_out))
    stats_out = output_forward(product_out, out_weights[0], norm_gains[0, 1], norm_shifts[0, 1])
    middle = (pair_float + saved_out[6] * stats_out[0]).astype(jnp.bfloat16)
    left_in, right_in, saved_in = edges_forward(
        middle.astype(jnp.float32), edge_weights[1], norm_gains[1, 0], norm_shifts[1, 0]
    )
    product_in = product_of("ikc,kjc->ijc", transposed_rows(left_in), column_strip(right_in))
    stats_in = output_forward(product_in, out_weights[1], norm_gains[1, 1], norm_shifts[1, 1])
    upstream = pair_cotangent.astype(jnp.float32)
    grad_product_in, gate_in = output_backward(
        upstream, out_weights[1], norm_gains[1, 1], saved_in[6], stats_in
    )
    grad_left_in = product_of(
        "kjc,jic->kic", row_strip(right_in), transposed_columns(grad_product_in)
    )
    grad_right_in = product_of("kic,ijc->kjc", row_strip(left_in), column_strip(grad_product_in))
    grad_middle = upstream + edges_backward(
        grad_left_in, grad_right_in, gate_in, edge_weights[1], norm_gains[1, 0], saved_in
    )
    grad_product_out, gate_outer = output_backward(
        grad_middle, out_weights[0], norm_gains[0, 1], saved_out[6], stats_out
    )
    grad_left_out = product_of("ijc,jkc->ikc", row_strip(grad_product_out), strip_right)
    grad_right_out = product_of(
        "jic,ikc->jkc", transposed_rows(grad_product_out), column_strip(left_out)
    )
    pair_grad = grad_middle + edges_backward(
        grad_left_out, grad_right_out, gate_outer, edge_weights[0], norm_gains[0, 0], saved_out
    )
    edge_grads = jnp.stack([grad_left_out, grad_right_out, grad_left_in, grad_right_in])
    return (pair_grad.astype(jnp.bfloat16), edge_grads.astype(jnp.bfloat16))


def solution(mesh):
    return jax.shard_map(
        body,
        mesh=mesh,
        in_specs=(
            P(("groups", "row"), "col", None),
            P(("groups", "row"), "col", None),
            P(),
            P(),
            P(),
            P(),
        ),
        out_specs=(P(("groups", "row"), "col", None), P(None, ("groups", "row"), "col", None)),
        check_vma=False,
    )
```

profile of v0, /device:TPU:3, one launch (start us, length us, event | category | flops | bytes accessed | tf_op | source)
XLA Modules:
  0.0 212.6 jit_solution(16719749983396921521)
XLA Ops:
  3.8 1.2 fusion.8
  5.7 4.6 %all-to-all-start = ((bf16[16,16,128]{2,0,1:T(8,128)(2,1)}), bf16[16,16,128]{2,0,1:T(8,128)(2,1)S(1)}, u32[]{:S(2)}, u32[]{:S(2)}) async-start(bf16[16,16,128]{2,0,1:T(8,128)(2,1)} %copy.211), calls=%async_computation | async-start | bytes 131072 | tf_op jit(solution)/shard_map/all_to_all | solution.py:83
  10.3 6.6 %all_gather.37 = bf16[16,64,128]{2,1,0:T(8,128)(2,1)S(1)} all-gather(bf16[16,16,128]{2,1,0:T(8,128)(2,1)S(1)} %get-tuple-element.14), channel_id=1, replica_groups=mesh['groups'=2,'row'=4,'col'=4] {'col'}, dimensions={1}, use_global_device_ids=true | all-gather | bytes 327680 | tf_op jit(solution)/shard_map/all_gather | solution.py:75
  16.9 12.5 %all_gather.46 = bf16[64,16,128]{2,1,0:T(8,128)(2,1)S(1)} all-gather(bf16[16,16,128]{2,1,0:T(8,128)(2,1)S(1)} %get-tuple-element.14), channel_id=1, replica_groups=mesh['groups'=2,'row'=4,'col'=4] {'row'}, dimensions={0}, use_global_device_ids=true | all-gather | bytes 327680 | tf_op jit(solution)/shard_map/all_gather | solution.py:79
  30.1 5.6 %all-to-all-start.1 = ((bf16[64,4,128]{2,1,0:T(4,128)(2,1)}), bf16[64,4,128]{2,1,0:T(4,128)(2,1)S(1)}, u32[]{:S(2)}, u32[]{:S(2)}) async-start(bf16[64,4,128]{2,1,0:T(4,128)(2,1)} %copy.213), calls=%async_computation.1 | async-start | bytes 131072 | tf_op jit(solution)/shard_map/all_to_all | solution.py:87
  35.6 12.4 %all_gather.44 = bf16[64,16,128]{2,1,0:T(8,128)(2,1)S(1)} all-gather(bf16[16,16,128]{2,1,0:T(8,128)(2,1)S(1)} %get-tuple-element.15), channel_id=1, replica_groups=mesh['groups'=2,'row'=4,'col'=4] {'row'}, dimensions={0}, use_global_device_ids=true | all-gather | bytes 327680 | tf_op jit(solution)/shard_map/all_gather | solution.py:79
  49.0 1.3 copy.248
  50.3 10.9 %all_gather.36 = bf16[64,16,128]{2,1,0:T(8,128)(2,1)S(1)} all-gather(bf16[16,16,128]{2,1,0:T(8,128)(2,1)S(1)} %bitcast.239), channel_id=1, replica_groups=mesh['groups'=2,'row'=4,'col'=4] {'row'}, dimensions={0}, use_global_device_ids=true | all-gather | bytes 327680 | tf_op jit(solution)/shard_map/all_gather | solution.py:79
  65.8 8.9 %all-to-all-start.2 = ((bf16[16,16,128]{2,1,0:T(8,128)(2,1)}), bf16[16,16,128]{2,1,0:T(8,128)(2,1)S(1)}, u32[]{:S(2)}, u32[]{:S(2)}) async-start(bf16[16,16,128]{2,1,0:T(8,128)(2,1)} %get-tuple-element.12), calls=%async_computation.2 | async-start | bytes 131072 | tf_op jit(solution)/shard_map/all_to_all | solution.py:87
  74.7 6.2 %all_gather.43 = bf16[16,64,128]{2,1,0:T(8,128)(2,1)S(1)} all-gather(bf16[16,16,128]{2,1,0:T(8,128)(2,1)} %get-tuple-element.12), channel_id=1, replica_groups=mesh['groups'=2,'row'=4,'col'=4] {'col'}, dimensions={1}, use_global_device_ids=true | all-gather | bytes 327680 | tf_op jit(solution)/shard_map/all_gather | solution.py:75
  80.9 12.2 %all_gather.38 = bf16[64,16,128]{2,1,0:T(8,128)(2,1)S(1)} all-gather(bf16[16,16,128]{2,1,0:T(8,128)(2,1)S(1)} %get-tuple-element.13), channel_id=1, replica_groups=mesh['groups'=2,'row'=4,'col'=4] {'row'}, dimensions={0}, use_global_device_ids=true | all-gather | bytes 327680 | tf_op jit(solution)/shard_map/all_gather | solution.py:79
  93.6 1.2 copy.242
  95.5 3.7 %all-to-all-start.3 = ((bf16[4,64,128]{2,0,1:T(4,128)(2,1)}), bf16[4,64,128]{2,0,1:T(4,128)(2,1)S(1)}, u32[]{:S(2)}, u32[]{:S(2)}) async-start(bf16[4,64,128]{2,0,1:T(4,128)(2,1)} %copy.225), calls=%async_computation.3 | async-start | bytes 131072 | tf_op jit(solution)/shard_map/all_to_all | solution.py:83
  99.2 9.1 %all_gather.41 = bf16[16,64,128]{2,1,0:T(8,128)(2,1)S(1)} all-gather(bf16[16,16,128]{2,1,0:T(8,128)(2,1)S(1)} %get-tuple-element.13), channel_id=1, replica_groups=mesh['groups'=2,'row'=4,'col'=4] {'col'}, dimensions={1}, use_global_device_ids=true | all-gather | bytes 327680 | tf_op jit(solution)/shard_map/all_gather | solution.py:75
  109.6 5.9 %all_gather.39 = bf16[16,64,128]{2,0,1:T(8,128)(2,1)S(1)} all-gather(bf16[16,16,128]{2,0,1:T(8,128)(2,1)S(1)} %bitcast.240), channel_id=1, replica_groups=mesh['groups'=2,'row'=4,'col'=4] {'col'}, dimensions={1}, use_global_device_ids=true | all-gather | bytes 327680 | tf_op jit(solution)/shard_map/all_gather | solution.py:75
  115.4 1.3 copy.230
  116.8 1.4 fusion.128
  120.2 12.5 %all_gather.42 = bf16[64,16,128]{2,1,0:T(8,128)(2,1)S(1)} all-gather(bf16[16,16,128]{2,1,0:T(8,128)(2,1)S(1)} %multiply_convert_fusion.3), channel_id=1, replica_groups=mesh['groups'=2,'row'=4,'col'=4] {'row'}, dimensions={0}, use_global_device_ids=true | all-gather | bytes 327680 | tf_op jit(solution)/shard_map/all_gather | solution.py:79
  133.4 1.3 copy.241
  134.7 3.7 %all-to-all-start.4 = ((bf16[16,16,128]{2,0,1:T(8,128)(2,1)}), bf16[16,16,128]{2,0,1:T(8,128)(2,1)S(1)}, u32[]{:S(2)}, u32[]{:S(2)}) async-start(bf16[16,16,128]{2,0,1:T(8,128)(2,1)} %copy.232), calls=%async_computation.4 | async-start | bytes 131072 | tf_op jit(solution)/shard_map/all_to_all | solution.py:83
  138.4 1.6 fusion.130
  140.4 2.6 %all-to-all-done.4 = bf16[16,16,128]{2,0,1:T(8,128)(2,1)S(1)} async-done(((bf16[16,16,128]{2,0,1:T(8,128)(2,1)}), bf16[16,16,128]{2,0,1:T(8,128)(2,1)S(1)}, u32[]{:S(2)}, u32[]{:S(2)}) %all-to-all-start.4) | async-done | bytes 65568 | tf_op jit(solution)/shard_map/all_to_all | solution.py:83
  143.7 8.1 %all-to-all-start.5 = ((bf16[64,4,128]{2,1,0:T(4,128)(2,1)}), bf16[64,4,128]{2,1,0:T(4,128)(2,1)S(1)}, u32[]{:S(2)}, u32[]{:S(2)}) async-start(bf16[64,4,128]{2,1,0:T(4,128)(2,1)} %copy.234), calls=%async_computation.5 | async-start | bytes 131072 | tf_op jit(solution)/shard_map/all_to_all | solution.py:87
  153.6 11.3 %all_gather.40 = bf16[64,16,128]{2,1,0:T(8,128)(2,1)S(1)} all-gather(bf16[16,16,128]{2,1,0:T(8,128)(2,1)S(1)} %bitcast.241), channel_id=1, replica_groups=mesh['groups'=2,'row'=4,'col'=4] {'row'}, dimensions={0}, use_global_device_ids=true | all-gather | bytes 327680 | tf_op jit(solution)/shard_map/all_gather | solution.py:79
  164.9 1.3 copy.238
  166.2 1.6 fusion.129
  172.8 8.9 %all-to-all-start.6 = ((bf16[16,16,128]{2,1,0:T(8,128)(2,1)}), bf16[16,16,128]{2,1,0:T(8,128)(2,1)S(1)}, u32[]{:S(2)}, u32[]{:S(2)}) async-start(bf16[16,16,128]{2,1,0:T(8,128)(2,1)} %multiply_convert_fusion.1), calls=%async_computation.6 | async-start | bytes 131072 | tf_op jit(solution)/shard_map/all_to_all | solution.py:87
  181.7 6.3 %all_gather.45 = bf16[16,64,128]{2,1,0:T(8,128)(2,1)S(1)} all-gather(bf16[16,16,128]{2,1,0:T(8,128)(2,1)} %multiply_convert_fusion.1), channel_id=1, replica_groups=mesh['groups'=2,'row'=4,'col'=4] {'col'}, dimensions={1}, use_global_device_ids=true | all-gather | bytes 327680 | tf_op jit(solution)/shard_map/all_gather | solution.py:75
  189.2 1.4 fusion.131
  191.9 3.3 %all-to-all-start.7 = ((bf16[4,64,128]{2,0,1:T(4,128)(2,1)}), bf16[4,64,128]{2,0,1:T(4,128)(2,1)S(1)}, u32[]{:S(2)}, u32[]{:S(2)}) async-start(bf16[4,64,128]{2,0,1:T(4,128)(2,1)} %copy.252), calls=%async_computation.7 | async-start | bytes 131072 | tf_op jit(solution)/shard_map/all_to_all | solution.py:83
  195.2 4.6 %all-to-all-done.7 = bf16[4,64,128]{2,0,1:T(4,128)(2,1)S(1)} async-done(((bf16[4,64,128]{2,0,1:T(4,128)(2,1)}), bf16[4,64,128]{2,0,1:T(4,128)(2,1)S(1)}, u32[]{:S(2)}, u32[]{:S(2)}) %all-to-all-start.7) | async-done | bytes 65568 | tf_op jit(solution)/shard_map/all_to_all | solution.py:83
  199.9 6.9 %all_gather.47 = bf16[16,64,128]{2,0,1:T(8,128)(2,1)S(1)} all-gather(bf16[16,16,128]{2,0,1:T(8,128)(2,1)S(1)} %bitcast.242), channel_id=1, replica_groups=mesh['groups'=2,'row'=4,'col'=4] {'col'}, dimensions={1}, use_global_device_ids=true | all-gather | bytes 327680 | tf_op jit(solution)/shard_map/all_gather | solution.py:75
  (179 shorter events, 31.0 us)
Async XLA Ops:
  0.6 1.0 copy-start.3
  1.7 1.5 copy-start.10
  2.6 2.4 %copy-start.13 = (f32[16,16]{1,0:T(8,128)}, f32[16,16]{1,0:T(8,128)S(1)}, u32[]{:S(2)}) copy-start(f32[16,16]{1,0:T(8,128)S(1)} %add_rsqrt_fusion.3) | copy-start | bytes 3076
  3.2 59.8 %copy-start.35 = (f32[128]{0:T(128)}, f32[128]{0:T(128)S(1)}, u32[]{:S(2)}) copy-start(f32[128]{0:T(128)S(1)} %get-tuple-element.33) | copy-start | bytes 1540
  3.2 61.5 %copy-start.31 = (f32[128]{0:T(128)}, f32[128]{0:T(128)S(1)}, u32[]{:S(2)}) copy-start(f32[128]{0:T(128)S(1)} %get-tuple-element.34) | copy-start | bytes 1540
  5.7 23.7 %all-to-all-start = ((bf16[16,16,128]{2,0,1:T(8,128)(2,1)}), bf16[16,16,128]{2,0,1:T(8,128)(2,1)S(1)}, u32[]{:S(2)}, u32[]{:S(2)}) async-start(bf16[16,16,128]{2,0,1:T(8,128)(2,1)} %copy.211), calls=%async_computation | async-start | bytes 131072 | tf_op jit(solution)/shard_map/all_to_all | solution.py:83
  30.1 20.2 %all-to-all-start.1 = ((bf16[64,4,128]{2,1,0:T(4,128)(2,1)}), bf16[64,4,128]{2,1,0:T(4,128)(2,1)S(1)}, u32[]{:S(2)}, u32[]{:S(2)}) async-start(bf16[64,4,128]{2,1,0:T(4,128)(2,1)} %copy.213), calls=%async_computation.1 | async-start | bytes 131072 | tf_op jit(solution)/shard_map/all_to_all | solution.py:87
  62.9 1.6 copy-start.23
  63.6 1.1 copy-start.5
  65.8 29.0 %all-to-all-start.2 = ((bf16[16,16,128]{2,1,0:T(8,128)(2,1)}), bf16[16,16,128]{2,1,0:T(8,128)(2,1)S(1)}, u32[]{:S(2)}, u32[]{:S(2)}) async-start(bf16[16,16,128]{2,1,0:T(8,128)(2,1)} %get-tuple-element.12), calls=%async_computation.2 | async-start | bytes 131072 | tf_op jit(solution)/shard_map/all_to_all | solution.py:87
  95.5 14.0 %all-to-all-start.3 = ((bf16[4,64,128]{2,0,1:T(4,128)(2,1)}), bf16[4,64,128]{2,0,1:T(4,128)(2,1)S(1)}, u32[]{:S(2)}, u32[]{:S(2)}) async-start(bf16[4,64,128]{2,0,1:T(4,128)(2,1)} %copy.225), calls=%async_computation.3 | async-start | bytes 131072 | tf_op jit(solution)/shard_map/all_to_all | solution.py:83
  118.8 1.2 copy-start.21
  118.8 0.9 copy-start.41
  119.0 1.0 copy-start.25
  134.7 8.3 %all-to-all-start.4 = ((bf16[16,16,128]{2,0,1:T(8,128)(2,1)}), bf16[16,16,128]{2,0,1:T(8,128)(2,1)S(1)}, u32[]{:S(2)}, u32[]{:S(2)}) async-start(bf16[16,16,128]{2,0,1:T(8,128)(2,1)} %copy.232), calls=%async_computation.4 | async-start | bytes 131072 | tf_op jit(solution)/shard_map/all_to_all | solution.py:83
  143.7 9.9 %all-to-all-start.5 = ((bf16[64,4,128]{2,1,0:T(4,128)(2,1)}), bf16[64,4,128]{2,1,0:T(4,128)(2,1)S(1)}, u32[]{:S(2)}, u32[]{:S(2)}) async-start(bf16[64,4,128]{2,1,0:T(4,128)(2,1)} %copy.234), calls=%async_computation.5 | async-start | bytes 131072 | tf_op jit(solution)/shard_map/all_to_all | solution.py:87
  169.3 1.0 copy-start.6
  169.3 1.0 copy-start.32
  170.8 1.1 copy-start.17
  172.8 18.4 %all-to-all-start.6 = ((bf16[16,16,128]{2,1,0:T(8,128)(2,1)}), bf16[16,16,128]{2,1,0:T(8,128)(2,1)S(1)}, u32[]{:S(2)}, u32[]{:S(2)}) async-start(bf16[16,16,128]{2,1,0:T(8,128)(2,1)} %multiply_convert_fusion.1), calls=%async_computation.6 | async-start | bytes 131072 | tf_op jit(solution)/shard_map/all_to_all | solution.py:87
  181.7 7.5 %copy-start = (bf16[64,16,128]{0,1,2:T(8,128)(2,1)S(1)}, bf16[64,16,128]{0,1,2:T(8,128)(2,1)}, u32[]{:S(2)}) copy-start(bf16[64,16,128]{0,1,2:T(8,128)(2,1)} %copy.248) | copy-start | bytes 786436
  191.2 4.1 %copy-start.27 = (bf16[16,16,640]{2,1,0:T(8,128)(2,1)}, bf16[16,16,640]{2,1,0:T(8,128)(2,1)S(1)}, u32[]{:S(2)}) copy-start(bf16[16,16,640]{2,1,0:T(8,128)(2,1)S(1)} %fusion.84) | copy-start | bytes 983044
  191.9 7.9 %all-to-all-start.7 = ((bf16[4,64,128]{2,0,1:T(4,128)(2,1)}), bf16[4,64,128]{2,0,1:T(4,128)(2,1)S(1)}, u32[]{:S(2)}, u32[]{:S(2)}) async-start(bf16[4,64,128]{2,0,1:T(4,128)(2,1)} %copy.252), calls=%async_computation.7 | async-start | bytes 131072 | tf_op jit(solution)/shard_map/all_to_all | solution.py:83
  207.7 1.0 copy-start.28
  208.7 0.9 copy-start.12
  208.7 0.9 copy-start.16
  208.7 0.9 copy-start.18
  208.8 1.1 copy-start.7
  209.6 0.9 copy-start.4
  209.6 0.9 copy-start.11
  209.6 0.9 copy-start.14
  210.9 1.0 copy-start.9
  (19 other events, 13.7 us)
where the time goes:
time: 215 us; the launch traced here: 213 us
  blocking collectives  113 us (53%)
  starting transfers between devices  46.7 us (22%)
  local copies, waits for them, and re-layouts  25.7 us (12%)
  matrix products  11 us (5%)
  waiting for transfers between devices  8.31 us (4%)
  other arithmetic  6.92 us (3%)
    all_gather x6, blocking collectives, column_strip(): return lax.all_gather(tile, 'row', axis=0, tiled=True)  71.8 us
    all_gather x6, blocking collectives, row_strip(): return lax.all_gather(tile, 'col', axis=1, tiled=True)  40.9 us
    all_to_all x4, starting transfers between devices, shuffle_columns(): return lax.all_to_all(tile, 'col', split_axis=0, concat_axis=1, tiled=True)  31.4 us
    all_to_all x4, starting transfers between devices, shuffle_rows(): return lax.all_to_all(tile, 'row', split_axis=1, concat_axis=0, tiled=True)  15.3 us
    dot_general x14, matrix products, product_of(): return jnp.einsum(form, left, right, preferred_element_type=jnp.float32)  11 us
    all_to_all x4, waiting for transfers between devices, shuffle_rows(): return lax.all_to_all(tile, 'row', split_axis=1, concat_axis=0, tiled=True)  7.18 us
    unnamed x86, local copies, waits for them, and re-layouts  6.71 us
  transfers between devices with their start and end apart: 8, of which 3 were waited for; matrix products, arithmetic and copies ran while one was open for 5% of the time, Pallas kernels for 0%

commit v1 on v0

--- a/solution.py
+++ b/solution.py
@@ -1,6 +1,10 @@
+import functools
+
 import jax
 import jax.numpy as jnp
 from jax import lax
+from jax.experimental import pallas as pl
+from jax.experimental.pallas import tpu as pltpu
 from jax.sharding import PartitionSpec as P
 
 EPSILON = 1e-05
@@ -113,7 +117,7 @@
     return jnp.swapaxes(gathered, 1, 2).reshape(gathered.shape[0], total, gathered.shape[4])
 
 
-def body(pair, pair_cotangent, edge_weights, out_weights, norm_gains, norm_shifts):
+def gathered_body(pair, pair_cotangent, edge_weights, out_weights, norm_gains, norm_shifts):
     pair_float = pair.astype(jnp.float32)
     left_out, right_out, saved_out = edges_forward(
         pair_float, edge_weights[0], norm_gains[0, 0], norm_shifts[0, 0]
@@ -150,6 +154,445 @@
     )
     edge_grads = jnp.stack([grad_left_out, grad_right_out, grad_left_in, grad_right_in])
     return (pair_grad.astype(jnp.bfloat16), edge_grads.astype(jnp.bfloat16))
+
+
+MESH = pl.DeviceIdType.MESH
+LEFT_OUT, RIGHT_OUT, LEFT_IN, RIGHT_IN = range(4)
+STANDARD, VALUE_LEFT, SIGMA_LEFT, VALUE_RIGHT, SIGMA_RIGHT, GATE, HIDDEN, CENTRED = range(8)
+
+
+def matmul(left, right):
+    return jnp.dot(left, right, preferred_element_type=jnp.float32)
+
+
+def matmul_transposed(left, right):
+    return lax.dot_general(
+        left, right, (((1,), (1,)), ((), ())), preferred_element_type=jnp.float32
+    )
+
+
+def kernel(
+    parts,
+    side,
+    pair_ref,
+    cotangent_ref,
+    edge_weights_ref,
+    out_weights_ref,
+    gains_ref,
+    shifts_ref,
+    pair_grad_ref,
+    edge_grads_ref,
+    own,
+    strips,
+    partials,
+    sums,
+    wide,
+    saved,
+    inverses,
+    projected,
+    work,
+    grads,
+    middle,
+    upstream,
+    pieces,
+    strip_send,
+    strip_recv,
+    sum_send,
+    sum_recv,
+):
+    row = lax.axis_index("row")
+    col = lax.axis_index("col")
+    area = side * side
+    diagonal = row == col
+    chunk = min(area, 64)
+
+    def turned(index, step):
+        return lax.rem(index + step, parts)
+
+    barrier = pltpu.get_barrier_semaphore()
+    me = row * parts + col
+    others = parts * parts - 1
+
+    def greet(step, carry):
+        other = lax.rem(me + step, parts * parts)
+        pl.semaphore_signal(
+            barrier,
+            inc=1,
+            device_id={"row": other // parts, "col": lax.rem(other, parts)},
+            device_id_type=MESH,
+        )
+        return carry
+
+    lax.fori_loop(1, others + 1, greet, 0)
+
+    def in_chunks(step):
+        def run(index, carry):
+            step(pl.ds(pl.multiple_of(index * chunk, chunk), chunk))
+            return carry
+
+        lax.fori_loop(0, area // chunk, run, 0)
+
+    def remote(source, target, send_sem, recv_sem, device):
+        return pltpu.make_async_remote_copy(
+            src_ref=source,
+            dst_ref=target,
+            send_sem=send_sem,
+            recv_sem=recv_sem,
+            device_id={"row": device[0], "col": device[1]},
+            device_id_type=MESH,
+        )
+
+    def route(kind, step):
+        if kind == "row":
+            return (row, turned(col, step)), turned(col, step), col
+        if kind == "col":
+            return (turned(row, step), col), turned(row, step), row
+        if kind == "to_col":
+            return (turned(row, step), row), turned(row, step), col
+        return (col, turned(col, step)), turned(col, step), row
+
+    def ship(kind, step, source, buffer, which, send_sems, recv_sems):
+        device, _, slot = route(kind, step)
+        copy = remote(
+            source,
+            buffer.at[which, slot],
+            send_sems.at[which, step],
+            recv_sems.at[which, slot],
+            device,
+        )
+        if step > 0:
+            copy.start()
+            return
+        local = pltpu.make_async_copy(source, buffer.at[which, slot], recv_sems.at[which, slot])
+        if kind in ("row", "col"):
+            local.start()
+        else:
+            pl.when(diagonal)(local.start)
+            pl.when(jnp.logical_not(diagonal))(copy.start)
+
+    def shipped(kind, step, source, buffer, which, send_sems, recv_sems):
+        device, _, slot = route(kind, step)
+        copy = remote(
+            source,
+            buffer.at[which, slot],
+            send_sems.at[which, step],
+            recv_sems.at[which, slot],
+            device,
+        )
+        if step > 0:
+            copy.wait_send()
+        elif kind not in ("row", "col"):
+            pl.when(jnp.logical_not(diagonal))(copy.wait_send)
+
+    def landed(buffer, which, slot, send_sems, recv_sems):
+        remote(
+            buffer.at[which, slot],
+            buffer.at[which, slot],
+            send_sems.at[which, 0],
+            recv_sems.at[which, slot],
+            (row, col),
+        ).wait_recv()
+
+    def project(update, source, cast):
+        gain = gains_ref[update, 0:1, :]
+        shift = shifts_ref[update, 0:1, :]
+
+        def norm_step(rows):
+            inputs = source[rows, :].astype(jnp.float32)
+            standard, inverse, normed = layer_norm(inputs, gain, shift)
+            saved[update, STANDARD, rows, :] = standard
+            inverses[update, 0, rows, :] = jnp.broadcast_to(inverse, standard.shape)
+            cast[rows, :] = normed.astype(jnp.bfloat16)
+
+        in_chunks(norm_step)
+        projected[...] = matmul(cast[...], edge_weights_ref[update])
+
+        def gate_step(rows):
+            width = gain.shape[1]
+            value_left = projected[rows, 0:width]
+            sigma_left = jax.nn.sigmoid(projected[rows, width : 2 * width])
+            value_right = projected[rows, 2 * width : 3 * width]
+            sigma_right = jax.nn.sigmoid(projected[rows, 3 * width : 4 * width])
+            own[2 * update, rows, :] = (sigma_left * value_left).astype(jnp.bfloat16)
+            own[2 * update + 1, rows, :] = (sigma_right * value_right).astype(jnp.bfloat16)
+            saved[update, VALUE_LEFT, rows, :] = value_left
+            saved[update, SIGMA_LEFT, rows, :] = sigma_left
+            saved[update, VALUE_RIGHT, rows, :] = value_right
+            saved[update, SIGMA_RIGHT, rows, :] = sigma_right
+            saved[update, GATE, rows, :] = jax.nn.sigmoid(projected[rows, 4 * width :])
+
+        in_chunks(gate_step)
+
+    def widen(which, slot):
+        landed(strips, which, slot, strip_send, strip_recv)
+
+        def step(rows):
+            wide[which, slot, rows, :] = strips[which, slot, rows, :].astype(jnp.float32)
+
+        in_chunks(step)
+
+    def contract(totals, spread, spread_major, stream, stream_major):
+        half = 8
+
+        def run(index, totals):
+            totals = list(totals)
+            for inner in range(half):
+                t = index * half + inner
+                if stream_major:
+                    block = stream[pl.ds(pl.multiple_of(t * side, side), side), :]
+                else:
+                    block = stream[pl.ds(t, side, stride=side), :]
+                for a in range(side):
+                    place = t * side + a if spread_major else a * side + t
+                    totals[a] = totals[a] + spread[pl.ds(place, 1), :] * block
+            return tuple(totals)
+
+        return lax.fori_loop(0, side // half, run, totals)
+
+    def zeros():
+        return tuple(jnp.zeros((side, pair_ref.shape[-1]), jnp.float32) for _ in range(side))
+
+    def product(left, right, start, left_major, right_major):
+        for a in range(side):
+            work[a * side : (a + 1) * side, :] = jnp.zeros((side, work.shape[1]), jnp.float32)
+        def step(index, carry):
+            slot = turned(start, index)
+            widen(left, slot)
+            widen(right, slot)
+            totals = tuple(work[a * side : (a + 1) * side, :] for a in range(side))
+            totals = contract(
+                totals, wide.at[left, slot], left_major, wide.at[right, slot], right_major
+            )
+            for a in range(side):
+                work[a * side : (a + 1) * side, :] = totals[a]
+            return carry
+
+        lax.fori_loop(0, parts, step, 0)
+
+    def output(update, cast):
+        gain = gains_ref[update, 1:2, :]
+        shift = shifts_ref[update, 1:2, :]
+
+        def norm_step(rows):
+            standard, inverse, normed = layer_norm(work[rows, :], gain, shift)
+            saved[update, CENTRED, rows, :] = standard
+            inverses[update, 1, rows, :] = jnp.broadcast_to(inverse, standard.shape)
+            cast[rows, :] = normed.astype(jnp.bfloat16)
+
+        in_chunks(norm_step)
+        saved[update, HIDDEN] = matmul(cast[...], out_weights_ref[update])
+
+    def output_back(update, cast):
+        gain = gains_ref[update, 1:2, :]
+        width = gain.shape[1]
+
+        def gate_step(rows):
+            incoming = upstream[rows, :]
+            gate = saved[update, GATE, rows, :]
+            gated = incoming * gate
+            cast[rows, :] = gated.astype(jnp.bfloat16)
+            term = gated * saved[update, HIDDEN, rows, :] * (1.0 - gate)
+            pieces[rows, 4 * width :] = term.astype(jnp.bfloat16)
+
+        in_chunks(gate_step)
+        work[...] = matmul_transposed(cast[...], out_weights_ref[update])
+
+        def norm_step(rows):
+            grad = norm_backward(
+                work[rows, :],
+                saved[update, CENTRED, rows, :],
+                inverses[update, 1, rows, :],
+                gain,
+            )
+            work[rows, :] = grad.astype(jnp.bfloat16).astype(jnp.float32)
+
+        in_chunks(norm_step)
+
+    def partial(which, kind, operands):
+        def make(step):
+            _, tile, _ = route(kind, step)
+            totals = contract(zeros(), *operands(tile))
+            for a in range(side):
+                partials[which, tile, a * side : (a + 1) * side, :] = totals[a].astype(jnp.bfloat16)
+            ship(kind, step, partials.at[which, tile], sums, which, sum_send, sum_recv)
+
+        return make
+
+    def add_up(which):
+        for slot in range(parts):
+            landed(sums, which, slot, sum_send, sum_recv)
+
+        def step(rows):
+            total = sums[which, 0, rows, :].astype(jnp.float32)
+            for slot in range(1, parts):
+                total = total + sums[which, slot, rows, :].astype(jnp.float32)
+            grads[which % 2, rows, :] = total
+            edge_grads_ref[which, rows, :] = total.astype(jnp.bfloat16)
+
+        in_chunks(step)
+
+    def edges_back(update, finish):
+        gain = gains_ref[update, 0:1, :]
+        width = gain.shape[1]
+
+        def piece_step(rows):
+            for place, value, sigma in ((0, VALUE_LEFT, SIGMA_LEFT), (1, VALUE_RIGHT, SIGMA_RIGHT)):
+                gate = saved[update, sigma, rows, :]
+                scaled = grads[place, rows, :] * gate
+                start = 2 * place * width
+                pieces[rows, start : start + width] = scaled.astype(jnp.bfloat16)
+                slope = scaled * saved[update, value, rows, :] * (1.0 - gate)
+                pieces[rows, start + width : start + 2 * width] = slope.astype(jnp.bfloat16)
+
+        in_chunks(piece_step)
+        work[...] = matmul_transposed(pieces[...], edge_weights_ref[update])
+
+        def norm_step(rows):
+            finish(
+                rows,
+                norm_backward(
+                    work[rows, :],
+                    saved[update, STANDARD, rows, :],
+                    inverses[update, 0, rows, :],
+                    gain,
+                ),
+            )
+
+        in_chunks(norm_step)
+
+    def spread_strip(which, kind):
+        for step in range(parts):
+            ship(kind, step, own.at[which], strips, which, strip_send, strip_recv)
+
+    cast = middle.at[1]
+    project(0, pair_ref, cast)
+    pl.semaphore_wait(barrier, others)
+    spread_strip(LEFT_OUT, "row")
+    spread_strip(RIGHT_OUT, "to_col")
+    product(LEFT_OUT, RIGHT_OUT, col, False, False)
+    output(0, cast)
+
+    def middle_step(rows):
+        update = saved[0, GATE, rows, :] * saved[0, HIDDEN, rows, :]
+        middle[0, rows, :] = (pair_ref[rows, :].astype(jnp.float32) + update).astype(jnp.bfloat16)
+        upstream[rows, :] = cotangent_ref[rows, :].astype(jnp.float32)
+
+    in_chunks(middle_step)
+
+    project(1, middle.at[0], cast)
+    spread_strip(LEFT_IN, "to_row")
+    spread_strip(RIGHT_IN, "col")
+    product(LEFT_IN, RIGHT_IN, row, True, True)
+    output(1, cast)
+    output_back(1, cast)
+
+    make_left = partial(
+        LEFT_IN, "to_col", lambda tile: (wide.at[RIGHT_IN, tile], False, work, False)
+    )
+    make_right = partial(
+        RIGHT_IN, "col", lambda tile: (wide.at[LEFT_IN, tile], False, work, True)
+    )
+    for step in list(range(1, parts)) + [0]:
+        make_left(step)
+        make_right(step)
+    add_up(LEFT_IN)
+    add_up(RIGHT_IN)
+
+    def upstream_step(rows, grad):
+        upstream[rows, :] = upstream[rows, :] + grad
+
+    edges_back(1, upstream_step)
+    output_back(0, cast)
+
+    make_left = partial(
+        LEFT_OUT, "row", lambda tile: (work, False, wide.at[RIGHT_OUT, tile], True)
+    )
+    make_right = partial(
+        RIGHT_OUT, "to_row", lambda tile: (work, True, wide.at[LEFT_OUT, tile], True)
+    )
+    for step in list(range(1, parts)) + [0]:
+        make_left(step)
+        make_right(step)
+    add_up(LEFT_OUT)
+    add_up(RIGHT_OUT)
+
+    def final_step(rows, grad):
+        pair_grad_ref[rows, :] = (upstream[rows, :] + grad).astype(jnp.bfloat16)
+
+    edges_back(0, final_step)
+
+    strip_kinds = ("row", "to_col", "to_row", "col")
+    sum_kinds = ("row", "to_row", "to_col", "col")
+    for which in range(4):
+        for step in range(parts):
+            shipped(
+                strip_kinds[which], step, own.at[which], strips, which, strip_send, strip_recv
+            )
+            _, tile, _ = route(sum_kinds[which], step)
+            shipped(
+                sum_kinds[which],
+                step,
+                partials.at[which, tile],
+                sums,
+                which,
+                sum_send,
+                sum_recv,
+            )
+
+
+def fused_body(pair, pair_cotangent, edge_weights, out_weights, norm_gains, norm_shifts):
+    parts = lax.axis_size("row")
+    side, _, width = pair.shape
+    area = side * side
+    tile = (area, width)
+    vmem = pl.BlockSpec(memory_space=pltpu.VMEM)
+    pair_grad, edge_grads = pl.pallas_call(
+        functools.partial(kernel, parts, side),
+        out_shape=(
+            jax.ShapeDtypeStruct(tile, jnp.bfloat16),
+            jax.ShapeDtypeStruct((4, *tile), jnp.bfloat16),
+        ),
+        in_specs=[vmem] * 6,
+        out_specs=(vmem, vmem),
+        scratch_shapes=[
+            pltpu.VMEM((4, *tile), jnp.bfloat16),
+            pltpu.VMEM((4, parts, *tile), jnp.bfloat16),
+            pltpu.VMEM((4, parts, *tile), jnp.bfloat16),
+            pltpu.VMEM((4, parts, *tile), jnp.bfloat16),
+            pltpu.VMEM((4, parts, *tile), jnp.float32),
+            pltpu.VMEM((2, 8, *tile), jnp.float32),
+            pltpu.VMEM((2, 2, *tile), jnp.float32),
+            pltpu.VMEM((area, edge_weights.shape[2]), jnp.float32),
+            pltpu.VMEM(tile, jnp.float32),
+            pltpu.VMEM((2, *tile), jnp.float32),
+            pltpu.VMEM((2, *tile), jnp.bfloat16),
+            pltpu.VMEM(tile, jnp.float32),
+            pltpu.VMEM((area, edge_weights.shape[2]), jnp.bfloat16),
+            pltpu.SemaphoreType.DMA((4, parts)),
+            pltpu.SemaphoreType.DMA((4, parts)),
+            pltpu.SemaphoreType.DMA((4, parts)),
+            pltpu.SemaphoreType.DMA((4, parts)),
+        ],
+        compiler_params=pltpu.CompilerParams(
+            collective_id=0, has_side_effects=True, vmem_limit_bytes=40 * 1024 * 1024
+        ),
+    )(
+        pair.reshape(tile),
+        pair_cotangent.reshape(tile),
+        edge_weights,
+        out_weights,
+        norm_gains,
+        norm_shifts,
+    )
+    return pair_grad.reshape(pair.shape), edge_grads.reshape(4, *pair.shape)
+
+
+def body(pair, pair_cotangent, edge_weights, out_weights, norm_gains, norm_shifts):
+    arguments = (pair, pair_cotangent, edge_weights, out_weights, norm_gains, norm_shifts)
+    square = lax.axis_size("row") == lax.axis_size("col") and pair.shape[0] == pair.shape[1]
+    if square and pair.shape[0] % 16 == 0:
+        return fused_body(*arguments)
+    return gathered_body(*arguments)
 
 
 def solution(mesh):

time: 215 us -> 74.5 us (0.35)
  the two profiles are of different devices: /device:TPU:3 before, /device:TPU:0 now
where the time goes in v1:
time: 74.5 us; the launch traced here: 74.2 us
  Pallas kernels  67.3 us (90%)
  local copies, waits for them, and re-layouts  6.18 us (8%)
    pallas_call x1, Pallas kernels, fused_body(): pl.pallas_call(functools.partial(kernel, parts, side), out_shape=(jax.Sha...  67.3 us
    unnamed x14, local copies, waits for them, and re-layouts  6.18 us

profile of v1, /device:TPU:0, one launch (start us, length us, event | category | flops | bytes accessed | tf_op | source)
XLA Modules:
  0.0 74.2 jit_solution(10609075686539981302)
XLA Ops:
  0.6 0.0 copy-start.4
  0.6 0.7 copy-done.4
  1.3 0.0 copy-start
  1.3 1.0 %copy-done = bf16[2,128,640]{2,1,0:T(8,128)(2,1)S(1)} copy-done((bf16[2,128,640]{2,1,0:T(8,128)(2,1)S(1)}, bf16[2,128,640]{2,1,0:T(8,128)(2,1)}, u32[]{:S(2)}) %copy-start) | copy-done | bytes 327704
  2.3 0.0 copy-start.1
  2.3 0.8 %copy-done.1 = bf16[16,16,128]{2,1,0:T(8,128)(2,1)S(1)} copy-done((bf16[16,16,128]{2,1,0:T(8,128)(2,1)S(1)}, bf16[16,16,128]{2,1,0:T(8,128)(2,1)}, u32[]{:S(2)}) %copy-start.1) | copy-done | bytes 65560
  3.1 0.0 copy-start.2
  3.1 0.8 %copy-done.2 = bf16[16,16,128]{2,1,0:T(8,128)(2,1)S(1)} copy-done((bf16[16,16,128]{2,1,0:T(8,128)(2,1)S(1)}, bf16[16,16,128]{2,1,0:T(8,128)(2,1)}, u32[]{:S(2)}) %copy-start.2) | copy-done | bytes 65560
  4.0 0.0 copy-start.3
  4.0 0.8 %copy-done.3 = bf16[2,128,128]{2,1,0:T(8,128)(2,1)S(1)} copy-done((bf16[2,128,128]{2,1,0:T(8,128)(2,1)S(1)}, bf16[2,128,128]{2,1,0:T(8,128)(2,1)}, u32[]{:S(2)}) %copy-start.3) | copy-done | bytes 65560
  4.8 0.0 copy-start.5
  4.8 0.7 copy-done.5
  5.5 67.3 %shard_map.77 = (bf16[256,128]{1,0:T(8,128)(2,1)S(1)}, bf16[4,256,128]{2,1,0:T(8,128)(2,1)S(1)}) custom-call(bf16[256,128]{1,0:T(8,128)(2,1)S(1)} %bitcast.6, bf16[256,128]{1,0:T(8,128)(2,1)S(1)} %bitcast.7, bf16[2,128,640]{2,1,0:T(8,128)(2,1)S(1)} %copy-done, bf16[2,128,128]{2,1,0:T(8,128)(2,1)S(1)} %copy-done.3, f32[2,2,128]{2,1,0:T(2,128)S(1)} %copy-done.4, ...), custom_call_target="tpu_custom_call" | custom-call | tf_op jit(solution)/shard_map/pallas_call | solution.py:549
  72.8 0.6 copy.10
  73.5 0.7 copy.11
Async XLA Ops:
  0.6 0.7 copy-start.4
  1.3 1.0 %copy-start = (bf16[2,128,640]{2,1,0:T(8,128)(2,1)S(1)}, bf16[2,128,640]{2,1,0:T(8,128)(2,1)}, u32[]{:S(2)}) copy-start(bf16[2,128,640]{2,1,0:T(8,128)(2,1)} %edge_weights_ref.1) | copy-start | bytes 983044
  2.3 0.8 %copy-start.1 = (bf16[16,16,128]{2,1,0:T(8,128)(2,1)S(1)}, bf16[16,16,128]{2,1,0:T(8,128)(2,1)}, u32[]{:S(2)}) copy-start(bf16[16,16,128]{2,1,0:T(8,128)(2,1)} %param.6) | copy-start | bytes 196612
  3.1 0.8 %copy-start.2 = (bf16[16,16,128]{2,1,0:T(8,128)(2,1)S(1)}, bf16[16,16,128]{2,1,0:T(8,128)(2,1)}, u32[]{:S(2)}) copy-start(bf16[16,16,128]{2,1,0:T(8,128)(2,1)} %param.7) | copy-start | bytes 196612
  4.0 0.8 %copy-start.3 = (bf16[2,128,128]{2,1,0:T(8,128)(2,1)S(1)}, bf16[2,128,128]{2,1,0:T(8,128)(2,1)}, u32[]{:S(2)}) copy-start(bf16[2,128,128]{2,1,0:T(8,128)(2,1)} %out_weights_ref.1) | copy-start | bytes 196612
  4.8 0.7 copy-start.5

commit v2 on v0

--- a/solution.py
+++ b/solution.py
@@ -1,6 +1,10 @@
+import functools
+
 import jax
 import jax.numpy as jnp
 from jax import lax
+from jax.experimental import pallas as pl
+from jax.experimental.pallas import tpu as pltpu
 from jax.sharding import PartitionSpec as P
 
 EPSILON = 1e-05
@@ -113,7 +117,7 @@
     return jnp.swapaxes(gathered, 1, 2).reshape(gathered.shape[0], total, gathered.shape[4])
 
 
-def body(pair, pair_cotangent, edge_weights, out_weights, norm_gains, norm_shifts):
+def gathered_body(pair, pair_cotangent, edge_weights, out_weights, norm_gains, norm_shifts):
     pair_float = pair.astype(jnp.float32)
     left_out, right_out, saved_out = edges_forward(
         pair_float, edge_weights[0], norm_gains[0, 0], norm_shifts[0, 0]
@@ -150,6 +154,512 @@
     )
     edge_grads = jnp.stack([grad_left_out, grad_right_out, grad_left_in, grad_right_in])
     return (pair_grad.astype(jnp.bfloat16), edge_grads.astype(jnp.bfloat16))
+
+
+MESH = pl.DeviceIdType.MESH
+RIGHT_OUT, LEFT_IN, GRAD_IN, GRAD_OUT = range(4)
+PRODUCT_OUT, PRODUCT_IN, SUM_LEFT_IN, SUM_RIGHT_OUT = range(4)
+STRIP_AXIS = ("col", "row", "col", "row")
+SUM_AXIS = ("row", "col", "row", "col")
+STANDARD, VALUE_LEFT, SIGMA_LEFT, VALUE_RIGHT, SIGMA_RIGHT, GATE, CENTRED = range(7)
+
+
+def matmul(left, right):
+    return jnp.dot(left, right, preferred_element_type=jnp.float32)
+
+
+def matmul_transposed(left, right):
+    return lax.dot_general(
+        left, right, (((1,), (1,)), ((), ())), preferred_element_type=jnp.float32
+    )
+
+
+def kernel(
+    parts,
+    side,
+    pair_hbm,
+    cotangent_hbm,
+    edge_weights_hbm,
+    out_weights_hbm,
+    gains_hbm,
+    shifts_hbm,
+    pair_grad_ref,
+    edge_grads_ref,
+    pair_ref,
+    cotangent_ref,
+    edge_weights_ref,
+    out_weights_ref,
+    gains_ref,
+    shifts_ref,
+    own,
+    strips,
+    partials,
+    sums,
+    wide,
+    single,
+    saved,
+    inverses,
+    projected,
+    work,
+    extra,
+    grads,
+    middle,
+    cast,
+    upstream,
+    pieces,
+    load_sem,
+    strip_send,
+    strip_recv,
+    sum_send,
+    sum_recv,
+):
+    row = lax.axis_index("row")
+    col = lax.axis_index("col")
+    area = side * side
+    width = pair_ref.shape[1]
+    chunk = min(area, 64)
+    place_of = {"row": col, "col": row}
+
+    def turned(index, step):
+        return lax.rem(index + parts + step, parts)
+
+    def device_along(axis, place):
+        return {"row": row, "col": place} if axis == "row" else {"row": place, "col": col}
+
+    barrier = pltpu.get_barrier_semaphore()
+    for axis in ("row", "col"):
+        for step in range(1, parts):
+            pl.semaphore_signal(
+                barrier,
+                inc=1,
+                device_id=device_along(axis, turned(place_of[axis], step)),
+                device_id_type=MESH,
+            )
+
+    loads = [
+        pltpu.make_async_copy(source, target, load_sem.at[index])
+        for index, (source, target) in enumerate(
+            (
+                (pair_hbm, pair_ref),
+                (gains_hbm, gains_ref),
+                (shifts_hbm, shifts_ref),
+                (edge_weights_hbm, edge_weights_ref),
+                (out_weights_hbm, out_weights_ref),
+                (cotangent_hbm, cotangent_ref),
+            )
+        )
+    ]
+    for load in loads:
+        load.start()
+
+    def in_chunks(step):
+        def run(index, carry):
+            step(pl.ds(pl.multiple_of(index * chunk, chunk), chunk))
+            return carry
+
+        lax.fori_loop(0, area // chunk, run, 0)
+
+    def strip_copy(which, step):
+        axis = STRIP_AXIS[which]
+        return pltpu.make_async_remote_copy(
+            src_ref=own.at[which],
+            dst_ref=strips.at[which, place_of[axis]],
+            send_sem=strip_send.at[which, step],
+            recv_sem=strip_recv.at[which, place_of[axis]],
+            device_id=device_along(axis, turned(place_of[axis], step)),
+            device_id_type=MESH,
+        )
+
+    def send_strip(which):
+        for step in range(1, parts):
+            strip_copy(which, step).start()
+
+    def take_strip(which, slot):
+        pltpu.make_async_remote_copy(
+            src_ref=own.at[which],
+            dst_ref=strips.at[which, slot],
+            send_sem=strip_send.at[which, 0],
+            recv_sem=strip_recv.at[which, slot],
+            device_id=device_along("row", col),
+            device_id_type=MESH,
+        ).wait_recv()
+
+        def step(rows):
+            wide[which, slot, rows, :] = strips[which, slot, rows, :].astype(jnp.float32)
+
+        in_chunks(step)
+
+    def sum_copy(which, tile):
+        axis = SUM_AXIS[which]
+        return pltpu.make_async_remote_copy(
+            src_ref=partials.at[which, tile],
+            dst_ref=sums.at[which, place_of[axis]],
+            send_sem=sum_send.at[which, tile],
+            recv_sem=sum_recv.at[which, place_of[axis]],
+            device_id=device_along(axis, tile),
+            device_id_type=MESH,
+        )
+
+    def send_sum(which, tile, totals):
+        for a in range(side):
+            partials[which, tile, a * side : (a + 1) * side, :] = totals[a].astype(jnp.bfloat16)
+
+        @pl.when(tile != place_of[SUM_AXIS[which]])
+        def _():
+            sum_copy(which, tile).start()
+
+    def added(which):
+        place = place_of[SUM_AXIS[which]]
+        for step in range(1, parts):
+            slot = turned(place, -step)
+            pltpu.make_async_remote_copy(
+                src_ref=partials.at[which, 0],
+                dst_ref=sums.at[which, slot],
+                send_sem=sum_send.at[which, 0],
+                recv_sem=sum_recv.at[which, slot],
+                device_id=device_along("row", col),
+                device_id_type=MESH,
+            ).wait_recv()
+
+        def read(rows):
+            total = partials[which, place, rows, :].astype(jnp.float32)
+            for step in range(1, parts):
+                slot = turned(place, step)
+                total = total + sums[which, slot, rows, :].astype(jnp.float32)
+            return total
+
+        return read
+
+    def contract(totals, spread, spread_major, stream, stream_major):
+        half = 8
+
+        def run(index, totals):
+            totals = list(totals)
+            for inner in range(half):
+                t = index * half + inner
+                if stream_major:
+                    block = stream[pl.ds(pl.multiple_of(t * side, side), side), :]
+                else:
+                    block = stream[pl.ds(t, side, stride=side), :]
+                for a in range(side):
+                    place = t * side + a if spread_major else a * side + t
+                    totals[a] = totals[a] + spread[pl.ds(place, 1), :] * block
+            return tuple(totals)
+
+        return lax.fori_loop(0, side // half, run, totals)
+
+    def zeros():
+        return tuple(jnp.zeros((side, width), jnp.float32) for _ in range(side))
+
+    def over_strip(which, step):
+        place = place_of[STRIP_AXIS[which]]
+        step(place, True)
+
+        def run(index, carry):
+            slot = turned(place, -index)
+            take_strip(which, slot)
+            step(slot, False)
+            return carry
+
+        lax.fori_loop(1, parts, run, 0)
+
+    def put(target, totals):
+        for a in range(side):
+            target[a * side : (a + 1) * side, :] = totals[a]
+
+    def grow(target, first, operands):
+        totals = tuple(target[a * side : (a + 1) * side, :] for a in range(side))
+        if first:
+            totals = zeros()
+        put(target, contract(totals, *operands))
+
+    def norm_in(update, source):
+        gain = gains_ref[update, 0:1, :]
+        shift = shifts_ref[update, 0:1, :]
+
+        def step(rows):
+            inputs = source[rows, :].astype(jnp.float32)
+            standard, inverse, normed = layer_norm(inputs, gain, shift)
+            saved[update, STANDARD, rows, :] = standard
+            inverses[update, 0, rows, :] = jnp.broadcast_to(inverse, standard.shape)
+            cast[rows, :] = normed.astype(jnp.bfloat16)
+
+        in_chunks(step)
+
+    def project(update, start, stop):
+        projected[:, start:stop] = matmul(cast[...], edge_weights_ref[update, :, start:stop])
+
+    def edge(update, side_of, rows):
+        start = 2 * side_of * width
+        value = projected[rows, start : start + width]
+        sigma = jax.nn.sigmoid(projected[rows, start + width : start + 2 * width])
+        saved[update, VALUE_LEFT + 2 * side_of, rows, :] = value
+        saved[update, SIGMA_LEFT + 2 * side_of, rows, :] = sigma
+        return (sigma * value).astype(jnp.bfloat16)
+
+    def gate_out(update, rows):
+        gate = jax.nn.sigmoid(projected[rows, 4 * width :])
+        saved[update, GATE, rows, :] = gate
+
+    def pass_back(update):
+        def step(rows):
+            gated = upstream[rows, :] * saved[update, GATE, rows, :]
+            cast[rows, :] = gated.astype(jnp.bfloat16)
+
+        in_chunks(step)
+        work[...] = matmul_transposed(cast[...], out_weights_ref[update])
+
+    def product_back(update, which, rows, standard, inverse):
+        grad = norm_backward(work[rows, :], standard, inverse, gains_ref[update, 1:2, :])
+        grad = grad.astype(jnp.bfloat16)
+        own[which, rows, :] = grad
+        place = place_of[STRIP_AXIS[which]]
+        wide[which, place, rows, :] = grad.astype(jnp.float32)
+
+    def gate_piece(update, hidden):
+        def step(rows):
+            gate = saved[update, GATE, rows, :]
+            term = upstream[rows, :] * hidden[rows, :] * gate * (1.0 - gate)
+            pieces[rows, 4 * width :] = term.astype(jnp.bfloat16)
+
+        in_chunks(step)
+
+    def edge_pieces(update, side_of, rows, grad):
+        value = saved[update, VALUE_LEFT + 2 * side_of, rows, :]
+        sigma = saved[update, SIGMA_LEFT + 2 * side_of, rows, :]
+        scaled = grad * sigma
+        slope = scaled * value * (1.0 - sigma)
+        start = 2 * side_of * width
+        pieces[rows, start : start + width] = scaled.astype(jnp.bfloat16)
+        pieces[rows, start + width : start + 2 * width] = slope.astype(jnp.bfloat16)
+        edge_grads_ref[2 * update + side_of, rows, :] = grad.astype(jnp.bfloat16)
+
+    def pieces_back(update, start, stop):
+        return matmul_transposed(pieces[:, start:stop], edge_weights_ref[update, :, start:stop])
+
+    def input_back(update, rows):
+        return norm_backward(
+            work[rows, :],
+            saved[update, STANDARD, rows, :],
+            inverses[update, 0, rows, :],
+            gains_ref[update, 0:1, :],
+        )
+
+    for load in loads[:3]:
+        load.wait()
+    norm_in(0, pair_ref)
+    loads[3].wait()
+    project(0, 2 * width, 4 * width)
+
+    def right_out_step(rows):
+        right = edge(0, 1, rows)
+        own[RIGHT_OUT, rows, :] = right
+        wide[RIGHT_OUT, row, rows, :] = right.astype(jnp.float32)
+
+    in_chunks(right_out_step)
+    pl.semaphore_wait(barrier, 2 * (parts - 1))
+    send_strip(RIGHT_OUT)
+    project(0, 0, 2 * width)
+
+    def left_out_step(rows):
+        single[0, rows, :] = edge(0, 0, rows).astype(jnp.float32)
+
+    in_chunks(left_out_step)
+
+    def product_out_step(slot, first):
+        totals = contract(zeros(), single.at[0], False, wide.at[RIGHT_OUT, slot], False)
+        send_sum(PRODUCT_OUT, slot, totals)
+
+    over_strip(RIGHT_OUT, product_out_step)
+    project(0, 4 * width, 5 * width)
+    loads[4].wait()
+    loads[5].wait()
+
+    def gate_step(rows):
+        gate_out(0, rows)
+        upstream[rows, :] = cotangent_ref[rows, :].astype(jnp.float32)
+
+    in_chunks(gate_step)
+
+    total_out = added(PRODUCT_OUT)
+
+    def norm_out_step(rows):
+        standard, inverse, normed = layer_norm(
+            total_out(rows), gains_ref[0, 1:2, :], shifts_ref[0, 1:2, :]
+        )
+        saved[0, CENTRED, rows, :] = standard
+        inverses[0, 1, rows, :] = jnp.broadcast_to(inverse, standard.shape)
+        cast[rows, :] = normed.astype(jnp.bfloat16)
+
+    in_chunks(norm_out_step)
+    extra[0] = matmul(cast[...], out_weights_ref[0])
+
+    def middle_step(rows):
+        update = saved[0, GATE, rows, :] * extra[0, rows, :]
+        middle[rows, :] = (pair_ref[rows, :].astype(jnp.float32) + update).astype(jnp.bfloat16)
+
+    in_chunks(middle_step)
+
+    norm_in(1, middle)
+    project(1, 0, 2 * width)
+
+    def left_in_step(rows):
+        left = edge(1, 0, rows)
+        own[LEFT_IN, rows, :] = left
+        wide[LEFT_IN, col, rows, :] = left.astype(jnp.float32)
+
+    in_chunks(left_in_step)
+    send_strip(LEFT_IN)
+    project(1, 2 * width, 5 * width)
+
+    def right_in_step(rows):
+        single[1, rows, :] = edge(1, 1, rows).astype(jnp.float32)
+
+    in_chunks(right_in_step)
+
+    def product_in_step(slot, first):
+        totals = contract(zeros(), wide.at[LEFT_IN, slot], True, single.at[1], True)
+        send_sum(PRODUCT_IN, slot, totals)
+
+    over_strip(LEFT_IN, product_in_step)
+    in_chunks(functools.partial(gate_out, 1))
+    pass_back(1)
+
+    total_in = added(PRODUCT_IN)
+
+    def norm_in_step(rows):
+        standard, inverse, normed = layer_norm(
+            total_in(rows), gains_ref[1, 1:2, :], shifts_ref[1, 1:2, :]
+        )
+        cast[rows, :] = normed.astype(jnp.bfloat16)
+        product_back(1, GRAD_IN, rows, standard, inverse)
+
+    in_chunks(norm_in_step)
+    send_strip(GRAD_IN)
+    extra[1] = matmul(cast[...], out_weights_ref[1])
+    gate_piece(1, extra.at[1])
+
+    def left_in_back(slot, first):
+        totals = contract(zeros(), single.at[1], False, wide.at[GRAD_IN, slot], False)
+        send_sum(SUM_LEFT_IN, slot, totals)
+
+    over_strip(GRAD_IN, left_in_back)
+    for slot in range(parts):
+        grow(
+            grads,
+            slot == 0,
+            (wide.at[LEFT_IN, slot], False, wide.at[GRAD_IN, slot], True),
+        )
+    in_chunks(lambda rows: edge_pieces(1, 1, rows, grads[rows, :]))
+    work[...] = pieces_back(1, 2 * width, 5 * width)
+    sum_left_in = added(SUM_LEFT_IN)
+    in_chunks(lambda rows: edge_pieces(1, 0, rows, sum_left_in(rows)))
+    work[...] = work[...] + pieces_back(1, 0, 2 * width)
+
+    def grad_middle_step(rows):
+        upstream[rows, :] = upstream[rows, :] + input_back(1, rows)
+
+    in_chunks(grad_middle_step)
+
+    pass_back(0)
+
+    def product_out_back(rows):
+        product_back(0, GRAD_OUT, rows, saved[0, CENTRED, rows, :], inverses[0, 1, rows, :])
+
+    in_chunks(product_out_back)
+    send_strip(GRAD_OUT)
+    gate_piece(0, extra.at[0])
+
+    def right_out_back(slot, first):
+        totals = contract(zeros(), wide.at[GRAD_OUT, slot], True, single.at[0], True)
+        send_sum(SUM_RIGHT_OUT, slot, totals)
+
+    over_strip(GRAD_OUT, right_out_back)
+    for slot in range(parts):
+        grow(
+            grads,
+            slot == 0,
+            (wide.at[GRAD_OUT, slot], False, wide.at[RIGHT_OUT, slot], True),
+        )
+    in_chunks(lambda rows: edge_pieces(0, 0, rows, grads[rows, :]))
+    work[...] = pieces_back(0, 0, 2 * width) + pieces_back(0, 4 * width, 5 * width)
+    sum_right_out = added(SUM_RIGHT_OUT)
+    in_chunks(lambda rows: edge_pieces(0, 1, rows, sum_right_out(rows)))
+    work[...] = work[...] + pieces_back(0, 2 * width, 4 * width)
+
+    def final_step(rows):
+        total = upstream[rows, :] + input_back(0, rows)
+        pair_grad_ref[rows, :] = total.astype(jnp.bfloat16)
+
+    in_chunks(final_step)
+
+    for which in range(4):
+        for step in range(1, parts):
+            strip_copy(which, step).wait_send()
+            tile = turned(place_of[SUM_AXIS[which]], step)
+            sum_copy(which, tile).wait_send()
+
+
+def fused_body(pair, pair_cotangent, edge_weights, out_weights, norm_gains, norm_shifts):
+    parts = lax.axis_size("row")
+    side, _, width = pair.shape
+    area = side * side
+    tile = (area, width)
+    arguments = (
+        pair.reshape(tile),
+        pair_cotangent.reshape(tile),
+        edge_weights,
+        out_weights,
+        norm_gains,
+        norm_shifts,
+    )
+    vmem = pl.BlockSpec(memory_space=pltpu.VMEM)
+    semaphores = pltpu.SemaphoreType.DMA((4, parts))
+    pair_grad, edge_grads = pl.pallas_call(
+        functools.partial(kernel, parts, side),
+        out_shape=(
+            jax.ShapeDtypeStruct(tile, jnp.bfloat16),
+            jax.ShapeDtypeStruct((4, *tile), jnp.bfloat16),
+        ),
+        in_specs=[pl.BlockSpec(memory_space=pltpu.HBM)] * 6,
+        out_specs=(vmem, vmem),
+        scratch_shapes=[
+            *(pltpu.VMEM(argument.shape, argument.dtype) for argument in arguments),
+            pltpu.VMEM((4, *tile), jnp.bfloat16),
+            pltpu.VMEM((4, parts, *tile), jnp.bfloat16),
+            pltpu.VMEM((4, parts, *tile), jnp.bfloat16),
+            pltpu.VMEM((4, parts, *tile), jnp.bfloat16),
+            pltpu.VMEM((4, parts, *tile), jnp.float32),
+            pltpu.VMEM((2, *tile), jnp.float32),
+            pltpu.VMEM((2, 7, *tile), jnp.float32),
+            pltpu.VMEM((2, 2, *tile), jnp.float32),
+            pltpu.VMEM((area, edge_weights.shape[2]), jnp.float32),
+            pltpu.VMEM(tile, jnp.float32),
+            pltpu.VMEM((2, *tile), jnp.float32),
+            pltpu.VMEM(tile, jnp.float32),
+            pltpu.VMEM(tile, jnp.bfloat16),
+            pltpu.VMEM(tile, jnp.bfloat16),
+            pltpu.VMEM(tile, jnp.float32),
+            pltpu.VMEM((area, edge_weights.shape[2]), jnp.bfloat16),
+            pltpu.SemaphoreType.DMA((len(arguments),)),
+            semaphores,
+            semaphores,
+            semaphores,
+            semaphores,
+        ],
+        compiler_params=pltpu.CompilerParams(
+            collective_id=0, has_side_effects=True, vmem_limit_bytes=40 * 1024 * 1024
+        ),
+    )(*arguments)
+    return pair_grad.reshape(pair.shape), edge_grads.reshape(4, *pair.shape)
+
+
+def body(pair, pair_cotangent, edge_weights, out_weights, norm_gains, norm_shifts):
+    arguments = (pair, pair_cotangent, edge_weights, out_weights, norm_gains, norm_shifts)
+    square = lax.axis_size("row") == lax.axis_size("col") and pair.shape[0] == pair.shape[1]
+    if square and pair.shape[0] % 16 == 0:
+        return fused_body(*arguments)
+    return gathered_body(*arguments)
 
 
 def solution(mesh):

time: 215 us -> 55.7 us (0.26)
  blocking collectives: 113 us -> 0 us
  Pallas kernels: 0 us -> 48.5 us
  starting transfers between devices: 46.7 us -> 0 us
  local copies, waits for them, and re-layouts: 25.7 us -> 6.18 us
  matrix products: 11 us -> 0 us
  waiting for transfers between devices: 8.31 us -> 0 us
  other arithmetic: 6.92 us -> 0 us
    all_gather x12 -> x0, blocking collectives: 113 us -> none  [the longest x6 71.8 us: column_strip(): return lax.all_gather(tile, 'row', axis=0, tiled=True)]
    pallas_call x0 -> x1, Pallas kernels: none -> 48.5 us  [fused_body(): pl.pallas_call(functools.partial(kernel, parts, side), out_shape=(jax.Sha...]
    all_to_all x8 -> x0, starting transfers between devices: 46.7 us -> none  [the longest x4 31.4 us: shuffle_columns(): return lax.all_to_all(tile, 'col', split_axis=0, concat_axis=1, tiled=True)]
    dot_general x14 -> x0, matrix products: 11 us -> none  [product_of(): return jnp.einsum(form, left, right, preferred_element_type=jnp.float32)]
    all_to_all x8 -> x0, waiting for transfers between devices: 8.31 us -> none  [the longest x4 7.18 us: shuffle_rows(): return lax.all_to_all(tile, 'row', split_axis=1, concat_axis=0, tiled=True)]
    all_gather x8 -> x0, local copies, waits for them, and re-layouts: 7.72 us -> none  [the longest x4 4.03 us: row_strip(): return lax.all_gather(tile, 'col', axis=1, tiled=True)]
    reshape x4 -> x0, local copies, waits for them, and re-layouts: 3.71 us -> none  [the longest x2 1.86 us: transposed_rows(): jnp.swapaxes(gathered, 1, 2)]
    all_to_all x16 -> x0, local copies, waits for them, and re-layouts: 2.82 us -> none  [the longest x8 1.41 us: shuffle_columns(): return lax.all_to_all(tile, 'col', split_axis=0, concat_axis=1, tiled=True)]
  transfers between devices with their start and end apart: 8 -> 0, of which waited for: 3 -> 0; matrix products, arithmetic and copies ran while one was open for 5% -> 0% of each run, Pallas kernels for 0% -> 0%
where the time goes in v2:
time: 55.7 us; the launch traced here: 55.3 us
  Pallas kernels  48.5 us (87%)
  local copies, waits for them, and re-layouts  6.18 us (11%)
  between operations  0.65 us (1%)
    pallas_call x1, Pallas kernels, fused_body(): pl.pallas_call(functools.partial(kernel, parts, side), out_shape=(jax.Sha...  48.5 us
    unnamed x14, local copies, waits for them, and re-layouts  6.18 us

profile of v2, /device:TPU:3, one launch (start us, length us, event | category | flops | bytes accessed | tf_op | source)
XLA Modules:
  0.0 55.3 jit_solution(25737598580358189)
XLA Ops:
  0.6 0.0 copy-start.4
  0.6 0.7 %copy-done.4 = f32[2,2,128]{2,1,0:T(2,128)S(1)} copy-done((f32[2,2,128]{2,1,0:T(2,128)S(1)}, f32[2,2,128]{2,1,0:T(2,128)}, u32[]{:S(2)}) %copy-start.4) | copy-done | bytes 2072
  1.3 0.0 copy-start
  1.3 1.0 %copy-done = bf16[2,128,640]{2,1,0:T(8,128)(2,1)S(1)} copy-done((bf16[2,128,640]{2,1,0:T(8,128)(2,1)S(1)}, bf16[2,128,640]{2,1,0:T(8,128)(2,1)}, u32[]{:S(2)}) %copy-start) | copy-done | bytes 327704
  2.3 0.0 copy-start.1
  2.3 0.8 %copy-done.1 = bf16[16,16,128]{2,1,0:T(8,128)(2,1)S(1)} copy-done((bf16[16,16,128]{2,1,0:T(8,128)(2,1)S(1)}, bf16[16,16,128]{2,1,0:T(8,128)(2,1)}, u32[]{:S(2)}) %copy-start.1) | copy-done | bytes 65560
  3.1 0.0 copy-start.2
  3.1 0.8 %copy-done.2 = bf16[16,16,128]{2,1,0:T(8,128)(2,1)S(1)} copy-done((bf16[16,16,128]{2,1,0:T(8,128)(2,1)S(1)}, bf16[16,16,128]{2,1,0:T(8,128)(2,1)}, u32[]{:S(2)}) %copy-start.2) | copy-done | bytes 65560
  4.0 0.0 copy-start.3
  4.0 0.8 %copy-done.3 = bf16[2,128,128]{2,1,0:T(8,128)(2,1)S(1)} copy-done((bf16[2,128,128]{2,1,0:T(8,128)(2,1)S(1)}, bf16[2,128,128]{2,1,0:T(8,128)(2,1)}, u32[]{:S(2)}) %copy-start.3) | copy-done | bytes 65560
  4.8 0.0 copy-start.5
  4.8 0.7 %copy-done.5 = f32[2,2,128]{2,1,0:T(2,128)S(1)} copy-done((f32[2,2,128]{2,1,0:T(2,128)S(1)}, f32[2,2,128]{2,1,0:T(2,128)}, u32[]{:S(2)}) %copy-start.5) | copy-done | bytes 2072
  5.5 48.5 %shard_map.77 = (bf16[256,128]{1,0:T(8,128)(2,1)S(1)}, bf16[4,256,128]{2,1,0:T(8,128)(2,1)S(1)}) custom-call(bf16[256,128]{1,0:T(8,128)(2,1)S(1)} %bitcast.6, bf16[256,128]{1,0:T(8,128)(2,1)S(1)} %bitcast.7, bf16[2,128,640]{2,1,0:T(8,128)(2,1)S(1)} %copy-done, bf16[2,128,128]{2,1,0:T(8,128)(2,1)S(1)} %copy-done.3, f32[2,2,128]{2,1,0:T(2,128)S(1)} %copy-done.4, ...), custom_call_target="tpu_custom_call" | custom-call | tf_op jit(solution)/shard_map/pallas_call | solution.py:618
  54.0 0.6 %copy.10 = bf16[16,16,128]{2,1,0:T(8,128)(2,1)} copy(bf16[16,16,128]{2,1,0:T(8,128)(2,1)S(1)} %bitcast.5) | data formatting | bytes 131072
  54.6 0.7 %copy.11 = bf16[4,16,16,128]{3,2,1,0:T(8,128)(2,1)} copy(bf16[4,16,16,128]{3,2,1,0:T(8,128)(2,1)S(1)} %bitcast.4) | data formatting | bytes 524288
Async XLA Ops:
  0.6 0.7 %copy-start.4 = (f32[2,2,128]{2,1,0:T(2,128)S(1)}, f32[2,2,128]{2,1,0:T(2,128)}, u32[]{:S(2)}) copy-start(f32[2,2,128]{2,1,0:T(2,128)} %gains_hbm.1) | copy-start | bytes 6148
  1.3 1.0 %copy-start = (bf16[2,128,640]{2,1,0:T(8,128)(2,1)S(1)}, bf16[2,128,640]{2,1,0:T(8,128)(2,1)}, u32[]{:S(2)}) copy-start(bf16[2,128,640]{2,1,0:T(8,128)(2,1)} %edge_weights_hbm.1) | copy-start | bytes 983044
  2.3 0.8 %copy-start.1 = (bf16[16,16,128]{2,1,0:T(8,128)(2,1)S(1)}, bf16[16,16,128]{2,1,0:T(8,128)(2,1)}, u32[]{:S(2)}) copy-start(bf16[16,16,128]{2,1,0:T(8,128)(2,1)} %param.6) | copy-start | bytes 196612
  3.1 0.8 %copy-start.2 = (bf16[16,16,128]{2,1,0:T(8,128)(2,1)S(1)}, bf16[16,16,128]{2,1,0:T(8,128)(2,1)}, u32[]{:S(2)}) copy-start(bf16[16,16,128]{2,1,0:T(8,128)(2,1)} %param.7) | copy-start | bytes 196612
  4.0 0.8 %copy-start.3 = (bf16[2,128,128]{2,1,0:T(8,128)(2,1)S(1)}, bf16[2,128,128]{2,1,0:T(8,128)(2,1)}, u32[]{:S(2)}) copy-start(bf16[2,128,128]{2,1,0:T(8,128)(2,1)} %out_weights_hbm.1) | copy-start | bytes 196612
  4.8 0.7 %copy-start.5 = (f32[2,2,128]{2,1,0:T(2,128)S(1)}, f32[2,2,128]{2,1,0:T(2,128)}, u32[]{:S(2)}) copy-start(f32[2,2,128]{2,1,0:T(2,128)} %shifts_hbm.1) | copy-start | bytes 6148

commit v3 on v2

--- a/solution.py
+++ b/solution.py
@@ -217,7 +217,7 @@
     col = lax.axis_index("col")
     area = side * side
     width = pair_ref.shape[1]
-    chunk = min(area, 64)
+    chunk = min(area, 128)
     place_of = {"row": col, "col": row}
 
     def turned(index, step):
@@ -253,11 +253,8 @@
         load.start()
 
     def in_chunks(step):
-        def run(index, carry):
-            step(pl.ds(pl.multiple_of(index * chunk, chunk), chunk))
-            return carry
-
-        lax.fori_loop(0, area // chunk, run, 0)
+        for start in range(0, area, chunk):
+            step(pl.ds(start, chunk))
 
     def strip_copy(which, step):
         axis = STRIP_AXIS[which]
@@ -648,7 +645,7 @@
             semaphores,
         ],
         compiler_params=pltpu.CompilerParams(
-            collective_id=0, has_side_effects=True, vmem_limit_bytes=40 * 1024 * 1024
+            collective_id=0, has_side_effects=True, vmem_limit_bytes=63 * 1024 * 1024
         ),
     )(*arguments)
     return pair_grad.reshape(pair.shape), edge_grads.reshape(4, *pair.shape)

time: 55.7 us -> 49.4 us (0.89)
  Pallas kernels: 48.5 us -> 45.4 us
  local copies, waits for them, and re-layouts: 6.18 us -> 3.14 us
    pallas_call x1, Pallas kernels: 48.5 us -> 45.4 us  [fused_body(): pl.pallas_call(functools.partial(kernel, parts, side), out_shape=(jax.Sha...]
    unnamed x14 -> x2, local copies, waits for them, and re-layouts: 6.18 us -> 3.14 us
where the time goes in v3:
time: 49.4 us; the launch traced here: 49.2 us
  Pallas kernels  45.4 us (92%)
  local copies, waits for them, and re-layouts  3.14 us (6%)
  between operations  0.64 us (1%)
    pallas_call x1, Pallas kernels, fused_body(): pl.pallas_call(functools.partial(kernel, parts, side), out_shape=(jax.Sha...  45.4 us
    unnamed x2, local copies, waits for them, and re-layouts  3.14 us

profile of v3, /device:TPU:3, one launch (start us, length us, event | category | flops | bytes accessed | tf_op | source)
XLA Modules:
  0.0 49.2 jit_solution(6587560765075454863)
XLA Ops:
  0.6 45.4 %shard_map.77 = (bf16[256,128]{1,0:T(8,128)(2,1)}, bf16[4,256,128]{2,1,0:T(8,128)(2,1)}) custom-call(bf16[256,128]{1,0:T(8,128)(2,1)} %bitcast.6, bf16[256,128]{1,0:T(8,128)(2,1)} %bitcast.7, bf16[2,128,640]{2,1,0:T(8,128)(2,1)} %edge_weights_hbm.1, bf16[2,128,128]{2,1,0:T(8,128)(2,1)} %out_weights_hbm.1, f32[2,2,128]{2,1,0:T(2,128)} %gains_hbm.1, ...), custom_call_target="tpu_custom_call" | custom-call | tf_op jit(solution)/shard_map/pallas_call | solution.py:615
  46.1 1.5 %copy.10 = bf16[16,16,128]{2,1,0:T(8,128)(2,1)} copy(bf16[16,16,128]{2,1,0:T(8,128)(2,1)} %bitcast.5) | data formatting | bytes 131072
  47.5 1.7 %copy.11 = bf16[4,16,16,128]{3,2,1,0:T(8,128)(2,1)} copy(bf16[4,16,16,128]{3,2,1,0:T(8,128)(2,1)} %bitcast.4) | data formatting | bytes 524288

commit v4 on v3

--- a/solution.py
+++ b/solution.py
@@ -183,6 +183,8 @@
     out_weights_hbm,
     gains_hbm,
     shifts_hbm,
+    pair_grad_hbm,
+    edge_grads_hbm,
     pair_grad_ref,
     edge_grads_ref,
     pair_ref,
@@ -208,6 +210,7 @@
     upstream,
     pieces,
     load_sem,
+    store_sem,
     strip_send,
     strip_recv,
     sum_send,
@@ -251,6 +254,11 @@
     ]
     for load in loads:
         load.start()
+    stores = [
+        pltpu.make_async_copy(edge_grads_ref.at[index], edge_grads_hbm.at[index], store_sem.at[index])
+        for index in range(4)
+    ]
+    stores.append(pltpu.make_async_copy(pair_grad_ref, pair_grad_hbm, store_sem.at[4]))
 
     def in_chunks(step):
         for start in range(0, area, chunk):
@@ -553,6 +561,9 @@
     in_chunks(lambda rows: edge_pieces(1, 0, rows, sum_left_in(rows)))
     work[...] = work[...] + pieces_back(1, 0, 2 * width)
 
+    stores[2].start()
+    stores[3].start()
+
     def grad_middle_step(rows):
         upstream[rows, :] = upstream[rows, :] + input_back(1, rows)
 
@@ -584,11 +595,17 @@
     in_chunks(lambda rows: edge_pieces(0, 1, rows, sum_right_out(rows)))
     work[...] = work[...] + pieces_back(0, 2 * width, 4 * width)
 
+    stores[0].start()
+    stores[1].start()
+
     def final_step(rows):
         total = upstream[rows, :] + input_back(0, rows)
         pair_grad_ref[rows, :] = total.astype(jnp.bfloat16)
 
     in_chunks(final_step)
+    stores[4].start()
+    for store in stores:
+        store.wait()
 
     for which in range(4):
         for step in range(1, parts):
@@ -610,7 +627,7 @@
         norm_gains,
         norm_shifts,
     )
-    vmem = pl.BlockSpec(memory_space=pltpu.VMEM)
+    hbm = pl.BlockSpec(memory_space=pltpu.HBM)
     semaphores = pltpu.SemaphoreType.DMA((4, parts))
     pair_grad, edge_grads = pl.pallas_call(
         functools.partial(kernel, parts, side),
@@ -618,9 +635,11 @@
             jax.ShapeDtypeStruct(tile, jnp.bfloat16),
             jax.ShapeDtypeStruct((4, *tile), jnp.bfloat16),
         ),
-        in_specs=[pl.BlockSpec(memory_space=pltpu.HBM)] * 6,
-        out_specs=(vmem, vmem),
+        in_specs=[hbm] * 6,
+        out_specs=(hbm, hbm),
         scratch_shapes=[
+            pltpu.VMEM(tile, jnp.bfloat16),
+            pltpu.VMEM((4, *tile), jnp.bfloat16),
             *(pltpu.VMEM(argument.shape, argument.dtype) for argument in arguments),
             pltpu.VMEM((4, *tile), jnp.bfloat16),
             pltpu.VMEM((4, parts, *tile), jnp.bfloat16),
@@ -639,6 +658,7 @@
             pltpu.VMEM(tile, jnp.float32),
             pltpu.VMEM((area, edge_weights.shape[2]), jnp.bfloat16),
             pltpu.SemaphoreType.DMA((len(arguments),)),
+            pltpu.SemaphoreType.DMA((5,)),
             semaphores,
             semaphores,
             semaphores,

time: 49.4 us -> 49.4 us (level)
  no operation moved by 1% of the time
where the time goes in v4:
time: 49.4 us; the launch traced here: 49.1 us
  Pallas kernels  45.4 us (92%)
  local copies, waits for them, and re-layouts  3.14 us (6%)
  between operations  0.64 us (1%)
    pallas_call x1, Pallas kernels, fused_body(): pl.pallas_call(functools.partial(kernel, parts, side), out_shape=(jax.Sha...  45.4 us
    unnamed x2, local copies, waits for them, and re-layouts  3.14 us

profile of v4, /device:TPU:3, one launch (start us, length us, event | category | flops | bytes accessed | tf_op | source)
XLA Modules:
  0.0 49.1 jit_solution(17061697447838986356)
XLA Ops:
  0.6 45.4 %shard_map.77 = (bf16[256,128]{1,0:T(8,128)(2,1)}, bf16[4,256,128]{2,1,0:T(8,128)(2,1)}) custom-call(bf16[256,128]{1,0:T(8,128)(2,1)} %bitcast.6, bf16[256,128]{1,0:T(8,128)(2,1)} %bitcast.7, bf16[2,128,640]{2,1,0:T(8,128)(2,1)} %edge_weights_hbm.1, bf16[2,128,128]{2,1,0:T(8,128)(2,1)} %out_weights_hbm.1, f32[2,2,128]{2,1,0:T(2,128)} %gains_hbm.1, ...), custom_call_target="tpu_custom_call" | custom-call | tf_op jit(solution)/shard_map/pallas_call | solution.py:632
  46.0 1.5 %copy.10 = bf16[16,16,128]{2,1,0:T(8,128)(2,1)} copy(bf16[16,16,128]{2,1,0:T(8,128)(2,1)} %bitcast.5) | data formatting | bytes 131072
  47.5 1.7 %copy.11 = bf16[4,16,16,128]{3,2,1,0:T(8,128)(2,1)} copy(bf16[4,16,16,128]{3,2,1,0:T(8,128)(2,1)} %bitcast.4) | data formatting | bytes 524288
